TPU v7x, 32 devices: a whole 2x2x4 slice. The times are simulated.
32 devices in a mesh: blk: 8 (over z, y), row: 4 (over x, core).
Axes of the slice: x: 2, y: 2, z: 4, core: 2. Of those that a mesh axis runs over, the one named last changes fastest.
Arguments:
- pool_embeds: bfloat16 [8192, 768], P('blk'), may hold values from -24 to 24
- target_samples: bfloat16 [2048, 768], P(('blk', 'row')), may hold values from -6 to 6
- reference_samples: bfloat16 [2048, 768], P(('blk', 'row')), may hold values from -6 to 6
Outputs:
- log_ratio: float32 [8192], P('blk')
- standardized: float32 [8192], P('blk')
All inputs are finite; a program needn't handle non-finite values.
Results may differ from a plain program's by a relative error of at most 0.0003.
Values may be sent and summed in bfloat16 or wider, within the bound.
A program may use at most 128 MiB of HBM per device.

v0:
```python
import functools
import math

import jax
import jax.numpy as jnp
from jax import lax
from jax.experimental import pallas as pl
from jax.experimental.pallas import tpu as pltpu
from jax.sharding import PartitionSpec as P

KERNEL_GAIN = 30.0
LOG2E = math.log2(math.e)
LN2 = math.log(2.0)
CHUNKS = 4
MESH = pl.DeviceIdType.MESH


def density_kernel(
    n_blk,
    n_row,
    pool_hbm,
    target_hbm,
    ref_hbm,
    target_out,
    ref_out,
    mean_out,
    scale_out,
    pool,
    other_pool,
    gathered,
    pool_norms,
    high,
    total,
    partials,
    outgoing,
    stats,
    load_sem,
    right_send,
    left_send,
    line_recv,
    cross_send,
    x_send,
    core_send,
    pool_recv,
    row_send,
    side_send,
    part_recv,
    stat_send,
    stat_recv,
):
    me = lax.axis_index("blk")
    my_row = lax.axis_index("row")
    length = n_blk // 2
    place = me // 2
    other = me + 1 - 2 * lax.rem(me, 2)
    core = lax.rem(my_row, 2)
    core_peer = my_row + 1 - 2 * core
    x_peers = [lax.rem(my_row + 2 * j, n_row) for j in range(1, n_row // 2)]
    row_peers = [lax.rem(my_row + i, n_row) for i in range(1, n_row)]
    rows, depth = pool.shape
    width = target_hbm.shape[0]
    chunk = other_pool.shape[2]
    factor = KERNEL_GAIN / depth * LOG2E
    sources = (target_hbm, ref_hbm)
    nt = (((1,), (1,)), ((), ()))

    pool_load = pltpu.make_async_copy(pool_hbm, pool, load_sem.at[2])
    pool_load.start()
    own_loads = [
        pltpu.make_async_copy(sources[k], gathered.at[place, k], load_sem.at[k]) for k in range(2)
    ]
    for load in own_loads:
        load.start()

    barrier = pltpu.get_barrier_semaphore()

    near = pl.semaphore_signal

    @pl.when(place < length - 1)
    def _():
        near(barrier, inc=1, device_id={"blk": me + 2}, device_id_type=MESH)

    @pl.when(place > 0)
    def _():
        near(barrier, inc=1, device_id={"blk": me - 2}, device_id_type=MESH)

    near(barrier, inc=1, device_id={"blk": other}, device_id_type=MESH)
    for peer in x_peers + [core_peer]:
        near(barrier, inc=1, device_id={"row": peer}, device_id_type=MESH)
    ends = (place == 0).astype(jnp.int32) + (place == length - 1).astype(jnp.int32)
    pl.semaphore_wait(barrier, 4 + len(x_peers) - ends)

    def line_copy(origin, k, src, step, sems):
        return pltpu.make_async_remote_copy(
            src_ref=src,
            dst_ref=gathered.at[origin, k],
            send_sem=sems.at[origin, k],
            recv_sem=line_recv.at[origin, k],
            device_id={"blk": me + 2 * step},
            device_id_type=MESH,
        )

    def cross_copy(c):
        at = pl.multiple_of((my_row * CHUNKS + c) * chunk, chunk)
        return pltpu.make_async_remote_copy(
            src_ref=pool_hbm.at[pl.ds(at, chunk)],
            dst_ref=other_pool.at[my_row, c],
            send_sem=cross_send.at[c],
            recv_sem=pool_recv.at[my_row, c],
            device_id={"blk": other},
            device_id_type=MESH,
        )

    def row_relay(quarter, c, peer, send_sem):
        return pltpu.make_async_remote_copy(
            src_ref=other_pool.at[quarter, c],
            dst_ref=other_pool.at[quarter, c],
            send_sem=send_sem,
            recv_sem=pool_recv.at[quarter, c],
            device_id={"row": peer},
            device_id_type=MESH,
        )

    def core_copy(quarter, c):
        return row_relay(quarter, c, core_peer, core_send.at[quarter, c])

    def x_copy(c, peer):
        return row_relay(my_row, c, peer, x_send.at[peer, c])

    for k in range(2):

        @pl.when(place < length - 1)
        def _(k=k):
            line_copy(place, k, sources[k], 1, right_send).start()

        @pl.when(place > 0)
        def _(k=k):
            line_copy(place, k, sources[k], -1, left_send).start()

    for c in range(CHUNKS):
        cross_copy(c).start()

    high[...] = jnp.full_like(high, -1e30)
    total[...] = jnp.zeros_like(total)

    def fold(origin, which, count=1):
        block = gathered[pl.ds(origin, count)].reshape(count * 2 * width, depth)
        columns = pool[...] if which == 0 else other_pool[...].reshape(rows, depth)
        norms = jnp.sum(jnp.square(block.astype(jnp.float32)), axis=1, keepdims=True) * factor
        products = lax.dot_general(block, columns, nt, preferred_element_type=jnp.float32)
        scores_all = products * (2.0 * factor) - norms
        for k in range(2):
            pieces = [scores_all[(2 * j + k) * width : (2 * j + k + 1) * width, :] for j in range(count)]
            at = 2 * which + k
            old = high[at : at + 1, :]
            best = [jnp.max(piece, axis=0, keepdims=True) for piece in pieces]
            new = functools.reduce(jnp.maximum, best, old)
            sums = [jnp.sum(jnp.exp2(piece - new), axis=0, keepdims=True) for piece in pieces]
            total[at : at + 1, :] = total[at : at + 1, :] * jnp.exp2(old - new) + sum(sums)
            high[at : at + 1, :] = new

    pool_load.wait()
    for load in own_loads:
        load.wait()
    fold(place, 0)

    ones = jnp.ones((8, depth), jnp.bfloat16)
    tile = 256 if rows % 256 == 0 else rows

    def norm_tile(i, carry):
        at = pl.multiple_of(i * tile, tile)
        squares = jnp.square(pool[pl.ds(at, tile), :].astype(jnp.float32))
        coarse = squares.astype(jnp.bfloat16)
        fine = (squares - coarse.astype(jnp.float32)).astype(jnp.bfloat16)
        sums = lax.dot_general(ones, coarse, nt, preferred_element_type=jnp.float32)
        sums = sums + lax.dot_general(ones, fine, nt, preferred_element_type=jnp.float32)
        pool_norms[:, pl.ds(at, tile)] = sums[0:1, :] * factor
        return carry

    line_ticks = 2 * (length - 1)
    ticks = max(line_ticks, CHUNKS + 2)

    def tick(i, carry):
        step = i // 2 + 1
        k = lax.rem(i, 2)

        @pl.when((i < line_ticks) & (place >= step))
        def _():
            origin = place - step
            block = gathered.at[origin, k]
            line_copy(origin, k, block, 1, right_send).wait_recv()

            @pl.when(place < length - 1)
            def _():
                line_copy(origin, k, block, 1, right_send).start()

        @pl.when((i < line_ticks) & (place + step < length))
        def _():
            origin = place + step
            block = gathered.at[origin, k]
            line_copy(origin, k, block, -1, left_send).wait_recv()

            @pl.when(place > 0)
            def _():
                line_copy(origin, k, block, -1, left_send).start()

        @pl.when(i < CHUNKS)
        def _():
            cross_copy(i).wait_recv()
            for peer in x_peers:
                x_copy(i, peer).start()
            core_copy(my_row, i).start()

        @pl.when((i >= 1) & (i <= CHUNKS))
        def _():
            for peer in x_peers:
                row_relay(peer, i - 1, peer, x_send.at[peer, i - 1]).wait_recv()
                core_copy(peer, i - 1).start()

        @pl.when(i < rows // tile)
        def _():
            norm_tile(i, 0)

        @pl.when((k == 1) & (place >= step) & (i < line_ticks - 1))
        def _():
            fold(place - step, 0)

        @pl.when((k == 1) & (place + step < length) & (i < line_ticks - 1))
        def _():
            fold(place + step, 0)

        @pl.when(i == ticks - 2)
        def _():
            for j in range(n_row // 2):
                quarter = lax.rem(core_peer + 2 * j, n_row)

                def arrived(c, carry, quarter=quarter):
                    core_copy(quarter, c).wait_recv()
                    return carry

                lax.fori_loop(0, CHUNKS, arrived, 0)

            first = jnp.minimum(place, 1)
            if length <= 4:
                fold(first, 1, length - 1)
            else:

                def early(origin, carry):
                    fold(origin, 1)
                    return carry

                lax.fori_loop(first, first + length - 1, early, 0)

            @pl.when((place > 0) & (place < length - 1))
            def _():
                fold(0, 1)

        return carry

    lax.fori_loop(0, ticks, tick, 0)
    lax.fori_loop(ticks, max(ticks, rows // tile), norm_tile, 0)

    @pl.when((place == 0) | (place == length - 1))
    def _():
        last = length - 1 - place
        fold(last, 0)
        fold(last, 1)

    logs = (high[...] + jnp.log2(total[...])) * LN2
    partials[my_row] = logs[0:2, :]
    outgoing[...] = logs[2:4, :]

    def row_copy(slot, peer):
        return pltpu.make_async_remote_copy(
            src_ref=partials.at[slot],
            dst_ref=partials.at[slot],
            send_sem=row_send.at[peer],
            recv_sem=part_recv.at[slot],
            device_id={"row": peer},
            device_id_type=MESH,
        )

    def side_copy(row, peer):
        return pltpu.make_async_remote_copy(
            src_ref=outgoing,
            dst_ref=partials.at[n_row + row],
            send_sem=side_send.at[peer],
            recv_sem=part_recv.at[n_row + row],
            device_id={"blk": other, "row": peer},
            device_id_type=MESH,
        )

    for peer in row_peers + [my_row]:
        side_copy(my_row, peer).start()
    for peer in row_peers:
        row_copy(my_row, peer).start()
    for peer in row_peers:
        row_copy(peer, peer).wait_recv()
    for peer in row_peers + [my_row]:
        side_copy(peer, peer).wait_recv()
    parts = [partials[i] for i in range(2 * n_row)]
    top = functools.reduce(jnp.maximum, parts)
    mass = functools.reduce(jnp.add, [jnp.exp(part - top) for part in parts])
    logs = top + jnp.log(mass) - pool_norms[...] * LN2
    ratio = logs[0:1, :] - logs[1:2, :]
    target_out[...] = logs[0:1, :]
    ref_out[...] = logs[1:2, :]

    local_mean = jnp.sum(ratio, axis=1, keepdims=True) / rows
    local_spread = jnp.sum(jnp.square(ratio - local_mean), axis=1, keepdims=True)
    lanes = stats.shape[2]
    stats[me, 0:1, :] = jnp.broadcast_to(local_mean, (1, lanes))
    stats[me, 1:2, :] = jnp.broadcast_to(local_spread, (1, lanes))

    def stat_copy(slot, peer):
        return pltpu.make_async_remote_copy(
            src_ref=stats.at[slot],
            dst_ref=stats.at[slot],
            send_sem=stat_send.at[peer],
            recv_sem=stat_recv.at[slot],
            device_id={"blk": peer},
            device_id_type=MESH,
        )

    def stat_start(i, carry):
        stat_copy(me, lax.rem(me + i, n_blk)).start()
        return carry

    def stat_wait(i, carry):
        peer = lax.rem(me + i, n_blk)
        stat_copy(peer, peer).wait_recv()
        return carry

    lax.fori_loop(1, n_blk, stat_start, 0)

    for k in range(2):

        def sent(origin, carry, k=k):
            @pl.when((origin <= place) & (place < length - 1))
            def _():
                line_copy(origin, k, gathered.at[origin, k], 1, right_send).wait_send()

            @pl.when((origin >= place) & (place > 0))
            def _():
                line_copy(origin, k, gathered.at[origin, k], -1, left_send).wait_send()

            return carry

        lax.fori_loop(0, length, sent, 0)

    def pool_sent(c, carry):
        cross_copy(c).wait_send()
        core_copy(my_row, c).wait_send()
        for peer in x_peers:
            x_copy(c, peer).wait_send()
            core_copy(peer, c).wait_send()
        return carry

    lax.fori_loop(0, CHUNKS, pool_sent, 0)
    for peer in row_peers:
        row_copy(my_row, peer).wait_send()
    for peer in row_peers + [my_row]:
        side_copy(my_row, peer).wait_send()

    lax.fori_loop(1, n_blk, stat_wait, 0)
    means = stats[:, 0, :]
    spreads = stats[:, 1, :]
    mean = jnp.sum(means, axis=0, keepdims=True) / n_blk
    spread = jnp.sum(spreads, axis=0, keepdims=True)
    spread = spread + rows * jnp.sum(jnp.square(means - mean), axis=0, keepdims=True)
    scale = jnp.sqrt(spread / (rows * n_blk) + 1e-05)
    mean_out[...] = jnp.broadcast_to(mean[:, 0:1], mean_out.shape)
    scale_out[...] = jnp.broadcast_to(scale[:, 0:1], scale_out.shape)

    def stat_sent(i, carry):
        stat_copy(me, lax.rem(me + i, n_blk)).wait_send()
        return carry

    lax.fori_loop(1, n_blk, stat_sent, 0)


def body(n_blk, n_row, pool_embeds, target_samples, reference_samples):
    rows, depth = pool_embeds.shape
    width = target_samples.shape[0]
    length = n_blk // 2
    dma = pltpu.SemaphoreType.DMA
    flops = 2 * rows * depth * 2 * width * n_blk
    log_target, log_ref, mean, scale = pl.pallas_call(
        functools.partial(density_kernel, n_blk, n_row),
        out_shape=[
            pltpu.VMEM((1, rows), jnp.float32),
            pltpu.VMEM((1, rows), jnp.float32),
            pltpu.VMEM((1, rows), jnp.float32),
            pltpu.VMEM((1, rows), jnp.float32),
        ],
        in_specs=[pl.BlockSpec(memory_space=pltpu.HBM)] * 3,
        out_specs=[pl.BlockSpec(memory_space=pltpu.VMEM)] * 4,
        scratch_shapes=[
            pltpu.VMEM((rows, depth), jnp.bfloat16),
            pltpu.VMEM((n_row, CHUNKS, rows // n_row // CHUNKS, depth), jnp.bfloat16),
            pltpu.VMEM((length, 2, width, depth), jnp.bfloat16),
            pltpu.VMEM((1, rows), jnp.float32),
            pltpu.VMEM((4, rows), jnp.float32),
            pltpu.VMEM((4, rows), jnp.float32),
            pltpu.VMEM((2 * n_row, 2, rows), jnp.float32),
            pltpu.VMEM((2, rows), jnp.float32),
            pltpu.VMEM((n_blk, 2, 128), jnp.float32),
            dma((3,)),
            dma((length, 2)),
            dma((length, 2)),
            dma((length, 2)),
            dma((CHUNKS,)),
            dma((n_row, CHUNKS)),
            dma((n_row, CHUNKS)),
            dma((n_row, CHUNKS)),
            dma((n_row,)),
            dma((n_row,)),
            dma((2 * n_row,)),
            dma((n_blk,)),
            dma((n_blk,)),
        ],
        compiler_params=pltpu.CompilerParams(
            collective_id=0, has_side_effects=True, vmem_limit_bytes=62 * 1024 * 1024
        ),
        cost_estimate=pl.CostEstimate(flops=flops, bytes_accessed=2 * rows * depth, transcendentals=0),
    )(pool_embeds, target_samples, reference_samples)
    ratio = log_target.reshape(rows) - log_ref.reshape(rows)
    return ratio, (ratio - mean.reshape(rows)) / scale.reshape(rows)


def solution(mesh):
    in_specs = (P("blk", None), P(("blk", "row"), None), P(("blk", "row"), None))
    out_specs = (P("blk"), P("blk"))
    part = functools.partial(body, mesh.shape["blk"], mesh.shape["row"])
    return jax.shard_map(part, mesh=mesh, in_specs=in_specs, out_specs=out_specs, check_vma=False)
```

profile of v0, /device:TPU:0, one launch (start us, length us, event | category | flops | bytes accessed | tf_op | source)
XLA Modules:
  0.0 32.8 jit_solution(2523572737853591976)
XLA Ops:
  0.6 31.5 %shard_map.50 = (f32[1,1024]{1,0:T(1,128)S(1)}, f32[1,1024]{1,0:T(1,128)S(1)}, f32[1,1024]{1,0:T(1,128)S(1)}, f32[1,1024]{1,0:T(1,128)S(1)}) custom-call(bf16[1024,768]{1,0:T(8,128)(2,1)} %pool_hbm.1, bf16[64,768]{1,0:T(8,128)(2,1)} %target_hbm.1, bf16[64,768]{1,0:T(8,128)(2,1)} %ref_hbm.1), custom_call_target="tpu_custom_call" | custom-call | flops 1610612736 | bytes 1572864 | tf_op jit(solution)/shard_map/pallas_call | solution.py:388
  32.1 0.0 copy-start
  32.2 0.6 %subtract_divide_fusion = f32[1024]{0:T(1024)} fusion(f32[1024]{0:T(1024)S(1)} %bitcast.4, f32[1024]{0:T(1024)S(1)} %bitcast.5, f32[1024]{0:T(1024)S(1)} %bitcast.3), kind=kLoop, calls=%fused_computation | loop fusion | flops 2048 | bytes 16384 | tf_op jit(solution)/shard_map/div | solution.py:428
  32.8 0.0 copy-done
  (1 shorter events, 0.0 us)
Async XLA Ops:
  32.1 0.6 %copy-start = (f32[1,1024]{1,0:T(1,128)}, f32[1,1024]{1,0:T(1,128)S(1)}, u32[]{:S(2)}) copy-start(f32[1,1024]{1,0:T(1,128)S(1)} %sub.9) | copy-start | bytes 12292
where the time goes:
time: 32.9 us; the launch traced here: 32.8 us
  Pallas kernels  31.5 us (96%)
  between operations  0.65 us (2%)
  other arithmetic  0.61 us (2%)
    pallas_call x1, Pallas kernels, body(): pl.pallas_call(functools.partial(density_kernel, n_blk, n_row), out_shape...  31.5 us

commit v1 on v0

--- a/solution.py
+++ b/solution.py
@@ -11,7 +11,7 @@
 KERNEL_GAIN = 30.0
 LOG2E = math.log2(math.e)
 LN2 = math.log(2.0)
-CHUNKS = 4
+CHUNKS = 2
 MESH = pl.DeviceIdType.MESH
 
 

time: 32.9 us -> 35.7 us (1.085)
  Pallas kernels: 31.5 us -> 34.3 us
    pallas_call x1, Pallas kernels: 31.5 us -> 34.3 us  [body(): pl.pallas_call(functools.partial(density_kernel, n_blk, n_row), out_shape...]
where the time goes in v1:
time: 35.7 us; the launch traced here: 35.5 us
  Pallas kernels  34.3 us (96%)
  between operations  0.65 us (2%)
  other arithmetic  0.61 us (2%)
    pallas_call x1, Pallas kernels, body(): pl.pallas_call(functools.partial(density_kernel, n_blk, n_row), out_shape...  34.3 us

profile of v1, /device:TPU:0, one launch (start us, length us, event | category | flops | bytes accessed | tf_op | source)
XLA Modules:
  0.0 35.5 jit_solution(2456178970145873433)
XLA Ops:
  0.6 34.3 %shard_map.50 = (f32[1,1024]{1,0:T(1,128)S(1)}, f32[1,1024]{1,0:T(1,128)S(1)}, f32[1,1024]{1,0:T(1,128)S(1)}, f32[1,1024]{1,0:T(1,128)S(1)}) custom-call(bf16[1024,768]{1,0:T(8,128)(2,1)} %pool_hbm.1, bf16[64,768]{1,0:T(8,128)(2,1)} %target_hbm.1, bf16[64,768]{1,0:T(8,128)(2,1)} %ref_hbm.1), custom_call_target="tpu_custom_call" | custom-call | flops 1610612736 | bytes 1572864 | tf_op jit(solution)/shard_map/pallas_call | solution.py:388
  34.9 0.0 copy-start
  34.9 0.6 %subtract_divide_fusion = f32[1024]{0:T(1024)} fusion(f32[1024]{0:T(1024)S(1)} %bitcast.4, f32[1024]{0:T(1024)S(1)} %bitcast.5, f32[1024]{0:T(1024)S(1)} %bitcast.3), kind=kLoop, calls=%fused_computation | loop fusion | flops 2048 | bytes 16384 | tf_op jit(solution)/shard_map/div | solution.py:428
  35.5 0.0 copy-done
  (1 shorter events, 0.0 us)
Async XLA Ops:
  34.9 0.6 %copy-start = (f32[1,1024]{1,0:T(1,128)}, f32[1,1024]{1,0:T(1,128)S(1)}, u32[]{:S(2)}) copy-start(f32[1,1024]{1,0:T(1,128)S(1)} %sub.9) | copy-start | bytes 12292

commit v2 on v0

--- a/solution.py
+++ b/solution.py
@@ -12,6 +12,7 @@
 LOG2E = math.log2(math.e)
 LN2 = math.log(2.0)
 CHUNKS = 4
+HALVES = 2
 MESH = pl.DeviceIdType.MESH
 
 
@@ -25,8 +26,7 @@
     ref_out,
     mean_out,
     scale_out,
-    pool,
-    other_pool,
+    pools,
     gathered,
     pool_norms,
     high,
@@ -57,14 +57,17 @@
     core_peer = my_row + 1 - 2 * core
     x_peers = [lax.rem(my_row + 2 * j, n_row) for j in range(1, n_row // 2)]
     row_peers = [lax.rem(my_row + i, n_row) for i in range(1, n_row)]
-    rows, depth = pool.shape
+    n_chunks = n_row * CHUNKS
+    chunk, depth = pools.shape[2:]
+    rows = n_chunks * chunk
+    half = rows // HALVES
+    per_half = n_chunks // HALVES
     width = target_hbm.shape[0]
-    chunk = other_pool.shape[2]
     factor = KERNEL_GAIN / depth * LOG2E
     sources = (target_hbm, ref_hbm)
     nt = (((1,), (1,)), ((), ()))
 
-    pool_load = pltpu.make_async_copy(pool_hbm, pool, load_sem.at[2])
+    pool_load = pltpu.make_async_copy(pool_hbm, pools.at[0], load_sem.at[2])
     pool_load.start()
     own_loads = [
         pltpu.make_async_copy(sources[k], gathered.at[place, k], load_sem.at[k]) for k in range(2)
@@ -101,10 +104,10 @@
         )
 
     def cross_copy(c):
-        at = pl.multiple_of((my_row * CHUNKS + c) * chunk, chunk)
-        return pltpu.make_async_remote_copy(
-            src_ref=pool_hbm.at[pl.ds(at, chunk)],
-            dst_ref=other_pool.at[my_row, c],
+        slot = c * n_row + my_row
+        return pltpu.make_async_remote_copy(
+            src_ref=pool_hbm.at[slot],
+            dst_ref=pools.at[1, slot],
             send_sem=cross_send.at[c],
             recv_sem=pool_recv.at[my_row, c],
             device_id={"blk": other},
@@ -113,8 +116,8 @@
 
     def row_relay(quarter, c, peer, send_sem):
         return pltpu.make_async_remote_copy(
-            src_ref=other_pool.at[quarter, c],
-            dst_ref=other_pool.at[quarter, c],
+            src_ref=pools.at[1, c * n_row + quarter],
+            dst_ref=pools.at[1, c * n_row + quarter],
             send_sem=send_sem,
             recv_sem=pool_recv.at[quarter, c],
             device_id={"row": peer},
@@ -143,33 +146,32 @@
     high[...] = jnp.full_like(high, -1e30)
     total[...] = jnp.zeros_like(total)
 
-    def fold(origin, which, count=1):
-        block = gathered[pl.ds(origin, count)].reshape(count * 2 * width, depth)
-        columns = pool[...] if which == 0 else other_pool[...].reshape(rows, depth)
+    def fold(origin, which, part):
+        block = gathered[origin].reshape(2 * width, depth)
+        columns = pools[which, pl.ds(part * per_half, per_half)].reshape(half, depth)
         norms = jnp.sum(jnp.square(block.astype(jnp.float32)), axis=1, keepdims=True) * factor
         products = lax.dot_general(block, columns, nt, preferred_element_type=jnp.float32)
         scores_all = products * (2.0 * factor) - norms
+        at = which * HALVES + part
         for k in range(2):
-            pieces = [scores_all[(2 * j + k) * width : (2 * j + k + 1) * width, :] for j in range(count)]
-            at = 2 * which + k
-            old = high[at : at + 1, :]
-            best = [jnp.max(piece, axis=0, keepdims=True) for piece in pieces]
-            new = functools.reduce(jnp.maximum, best, old)
-            sums = [jnp.sum(jnp.exp2(piece - new), axis=0, keepdims=True) for piece in pieces]
-            total[at : at + 1, :] = total[at : at + 1, :] * jnp.exp2(old - new) + sum(sums)
-            high[at : at + 1, :] = new
+            scores = scores_all[width * k : width * (k + 1), :]
+            old = high[at, k : k + 1, :]
+            new = jnp.maximum(old, jnp.max(scores, axis=0, keepdims=True))
+            summed = jnp.sum(jnp.exp2(scores - new), axis=0, keepdims=True)
+            total[at, k : k + 1, :] = total[at, k : k + 1, :] * jnp.exp2(old - new) + summed
+            high[at, k : k + 1, :] = new
 
     pool_load.wait()
     for load in own_loads:
         load.wait()
-    fold(place, 0)
 
     ones = jnp.ones((8, depth), jnp.bfloat16)
-    tile = 256 if rows % 256 == 0 else rows
+    tile = n_row * chunk
 
     def norm_tile(i, carry):
         at = pl.multiple_of(i * tile, tile)
-        squares = jnp.square(pool[pl.ds(at, tile), :].astype(jnp.float32))
+        block = pools[0, pl.ds(i * n_row, n_row)].reshape(tile, depth)
+        squares = jnp.square(block.astype(jnp.float32))
         coarse = squares.astype(jnp.bfloat16)
         fine = (squares - coarse.astype(jnp.float32)).astype(jnp.bfloat16)
         sums = lax.dot_general(ones, coarse, nt, preferred_element_type=jnp.float32)
@@ -221,54 +223,42 @@
         def _():
             norm_tile(i, 0)
 
-        @pl.when((k == 1) & (place >= step) & (i < line_ticks - 1))
-        def _():
-            fold(place - step, 0)
-
-        @pl.when((k == 1) & (place + step < length) & (i < line_ticks - 1))
-        def _():
-            fold(place + step, 0)
-
-        @pl.when(i == ticks - 2)
-        def _():
-            for j in range(n_row // 2):
-                quarter = lax.rem(core_peer + 2 * j, n_row)
-
-                def arrived(c, carry, quarter=quarter):
-                    core_copy(quarter, c).wait_recv()
+        for part in range(HALVES):
+
+            @pl.when(i == ticks - 1 - HALVES + part)
+            def _(part=part):
+                def arrived(c, carry):
+                    for j in range(n_row // 2):
+                        core_copy(lax.rem(core_peer + 2 * j, n_row), c).wait_recv()
                     return carry
 
-                lax.fori_loop(0, CHUNKS, arrived, 0)
-
-            first = jnp.minimum(place, 1)
-            if length <= 4:
-                fold(first, 1, length - 1)
-            else:
-
-                def early(origin, carry):
-                    fold(origin, 1)
-                    return carry
-
-                lax.fori_loop(first, first + length - 1, early, 0)
-
-            @pl.when((place > 0) & (place < length - 1))
+                each = CHUNKS // HALVES
+                lax.fori_loop(part * each, (part + 1) * each, arrived, 0)
+
+        def job(j, carry):
+            origin = lax.rem(j // HALVES, length)
+            part = lax.rem(j, HALVES)
+            which = j // (HALVES * length)
+            apart = jnp.maximum(origin - place, place - origin)
+            own_turn = jnp.maximum(2 * apart - 1, 0)
+            other_turn = jnp.where(apart < length - 1, ticks - 1 - HALVES + part, ticks - 1)
+            turn = jnp.where(which == 0, own_turn, other_turn)
+
+            @pl.when(turn == i)
             def _():
-                fold(0, 1)
-
+                fold(origin, which, part)
+
+            return carry
+
+        lax.fori_loop(0, 2 * length * HALVES, job, 0)
         return carry
 
     lax.fori_loop(0, ticks, tick, 0)
     lax.fori_loop(ticks, max(ticks, rows // tile), norm_tile, 0)
 
-    @pl.when((place == 0) | (place == length - 1))
-    def _():
-        last = length - 1 - place
-        fold(last, 0)
-        fold(last, 1)
-
     logs = (high[...] + jnp.log2(total[...])) * LN2
-    partials[my_row] = logs[0:2, :]
-    outgoing[...] = logs[2:4, :]
+    partials[my_row] = jnp.concatenate([logs[i] for i in range(HALVES)], axis=1)
+    outgoing[...] = jnp.concatenate([logs[HALVES + i] for i in range(HALVES)], axis=1)
 
     def row_copy(slot, peer):
         return pltpu.make_async_remote_copy(
@@ -383,6 +373,7 @@
     rows, depth = pool_embeds.shape
     width = target_samples.shape[0]
     length = n_blk // 2
+    chunk = rows // (n_row * CHUNKS)
     dma = pltpu.SemaphoreType.DMA
     flops = 2 * rows * depth * 2 * width * n_blk
     log_target, log_ref, mean, scale = pl.pallas_call(
@@ -396,12 +387,11 @@
         in_specs=[pl.BlockSpec(memory_space=pltpu.HBM)] * 3,
         out_specs=[pl.BlockSpec(memory_space=pltpu.VMEM)] * 4,
         scratch_shapes=[
-            pltpu.VMEM((rows, depth), jnp.bfloat16),
-            pltpu.VMEM((n_row, CHUNKS, rows // n_row // CHUNKS, depth), jnp.bfloat16),
+            pltpu.VMEM((2, n_row * CHUNKS, chunk, depth), jnp.bfloat16),
             pltpu.VMEM((length, 2, width, depth), jnp.bfloat16),
             pltpu.VMEM((1, rows), jnp.float32),
-            pltpu.VMEM((4, rows), jnp.float32),
-            pltpu.VMEM((4, rows), jnp.float32),
+            pltpu.VMEM((2 * HALVES, 2, rows // HALVES), jnp.float32),
+            pltpu.VMEM((2 * HALVES, 2, rows // HALVES), jnp.float32),
             pltpu.VMEM((2 * n_row, 2, rows), jnp.float32),
             pltpu.VMEM((2, rows), jnp.float32),
             pltpu.VMEM((n_blk, 2, 128), jnp.float32),
@@ -423,7 +413,7 @@
             collective_id=0, has_side_effects=True, vmem_limit_bytes=62 * 1024 * 1024
         ),
         cost_estimate=pl.CostEstimate(flops=flops, bytes_accessed=2 * rows * depth, transcendentals=0),
-    )(pool_embeds, target_samples, reference_samples)
+    )(pool_embeds.reshape(n_row * CHUNKS, chunk, depth), target_samples, reference_samples)
     ratio = log_target.reshape(rows) - log_ref.reshape(rows)
     return ratio, (ratio - mean.reshape(rows)) / scale.reshape(rows)
 

time: 32.9 us -> 36.4 us (1.11)
  Pallas kernels: 31.5 us -> 34.9 us
    pallas_call x1, Pallas kernels: 31.5 us -> 34.9 us  [body(): pl.pallas_call(functools.partial(density_kernel, n_blk, n_row), out_shape...]
where the time goes in v2:
time: 36.4 us; the launch traced here: 36.2 us
  Pallas kernels  34.9 us (96%)
  between operations  0.65 us (2%)
  other arithmetic  0.61 us (2%)
    pallas_call x1, Pallas kernels, body(): pl.pallas_call(functools.partial(density_kernel, n_blk, n_row), out_shape...  34.9 us

profile of v2, /device:TPU:0, one launch (start us, length us, event | category | flops | bytes accessed | tf_op | source)
XLA Modules:
  0.0 36.2 jit_solution(12369016188640608495)
XLA Ops:
  0.6 34.9 %shard_map.50 = (f32[1,1024]{1,0:T(1,128)S(1)}, f32[1,1024]{1,0:T(1,128)S(1)}, f32[1,1024]{1,0:T(1,128)S(1)}, f32[1,1024]{1,0:T(1,128)S(1)}) custom-call(bf16[16,64,768]{2,1,0:T(8,128)(2,1)} %bitcast.8, bf16[64,768]{1,0:T(8,128)(2,1)} %target_hbm.1, bf16[64,768]{1,0:T(8,128)(2,1)} %ref_hbm.1), custom_call_target="tpu_custom_call" | custom-call | flops 1610612736 | bytes 1572864 | tf_op jit(solution)/shard_map/pallas_call | solution.py:379
  35.6 0.0 copy-start
  35.6 0.6 %subtract_divide_fusion = f32[1024]{0:T(1024)} fusion(f32[1024]{0:T(1024)S(1)} %bitcast.5, f32[1024]{0:T(1024)S(1)} %bitcast.6, f32[1024]{0:T(1024)S(1)} %bitcast.4), kind=kLoop, calls=%fused_computation | loop fusion | flops 2048 | bytes 16384 | tf_op jit(solution)/shard_map/div | solution.py:418
  36.2 0.0 copy-done
  (1 shorter events, 0.0 us)
Async XLA Ops:
  35.6 0.6 %copy-start = (f32[1,1024]{1,0:T(1,128)}, f32[1,1024]{1,0:T(1,128)S(1)}, u32[]{:S(2)}) copy-start(f32[1,1024]{1,0:T(1,128)S(1)} %sub.9) | copy-start | bytes 12292

commit v3 on v0

--- a/solution.py
+++ b/solution.py
@@ -29,6 +29,7 @@
     other_pool,
     gathered,
     pool_norms,
+    sample_norms,
     high,
     total,
     partials,
@@ -58,6 +59,7 @@
     x_peers = [lax.rem(my_row + 2 * j, n_row) for j in range(1, n_row // 2)]
     row_peers = [lax.rem(my_row + i, n_row) for i in range(1, n_row)]
     rows, depth = pool.shape
+    lanes = stats.shape[2]
     width = target_hbm.shape[0]
     chunk = other_pool.shape[2]
     factor = KERNEL_GAIN / depth * LOG2E
@@ -143,10 +145,16 @@
     high[...] = jnp.full_like(high, -1e30)
     total[...] = jnp.zeros_like(total)
 
+    def set_norms(origin, k):
+        block = gathered[origin, k].astype(jnp.float32)
+        norms = jnp.sum(jnp.square(block), axis=1, keepdims=True) * factor
+        sample_norms[origin, k] = jnp.broadcast_to(norms, (width, lanes))
+
     def fold(origin, which, count=1):
         block = gathered[pl.ds(origin, count)].reshape(count * 2 * width, depth)
         columns = pool[...] if which == 0 else other_pool[...].reshape(rows, depth)
-        norms = jnp.sum(jnp.square(block.astype(jnp.float32)), axis=1, keepdims=True) * factor
+        norms = sample_norms[pl.ds(origin, count)].reshape(count * 2 * width, lanes)
+        norms = jnp.concatenate([norms] * (rows // lanes), axis=1)
         products = lax.dot_general(block, columns, nt, preferred_element_type=jnp.float32)
         scores_all = products * (2.0 * factor) - norms
         for k in range(2):
@@ -162,6 +170,8 @@
     pool_load.wait()
     for load in own_loads:
         load.wait()
+    for k in range(2):
+        set_norms(place, k)
     fold(place, 0)
 
     ones = jnp.ones((8, depth), jnp.bfloat16)
@@ -220,6 +230,17 @@
         @pl.when(i < rows // tile)
         def _():
             norm_tile(i, 0)
+
+        def norms_of(j, carry):
+            origin = place + (2 * j - 1) * step
+
+            @pl.when((i < line_ticks) & (origin >= 0) & (origin < length))
+            def _():
+                set_norms(origin, k)
+
+            return carry
+
+        lax.fori_loop(0, 2, norms_of, 0)
 
         @pl.when((k == 1) & (place >= step) & (i < line_ticks - 1))
         def _():
@@ -308,7 +329,6 @@
 
     local_mean = jnp.sum(ratio, axis=1, keepdims=True) / rows
     local_spread = jnp.sum(jnp.square(ratio - local_mean), axis=1, keepdims=True)
-    lanes = stats.shape[2]
     stats[me, 0:1, :] = jnp.broadcast_to(local_mean, (1, lanes))
     stats[me, 1:2, :] = jnp.broadcast_to(local_spread, (1, lanes))
 
@@ -400,6 +420,7 @@
             pltpu.VMEM((n_row, CHUNKS, rows // n_row // CHUNKS, depth), jnp.bfloat16),
             pltpu.VMEM((length, 2, width, depth), jnp.bfloat16),
             pltpu.VMEM((1, rows), jnp.float32),
+            pltpu.VMEM((length, 2, width, 128), jnp.float32),
             pltpu.VMEM((4, rows), jnp.float32),
             pltpu.VMEM((4, rows), jnp.float32),
             pltpu.VMEM((2 * n_row, 2, rows), jnp.float32),

time: 32.9 us -> 33.2 us (level)
  no operation moved by 1% of the time
where the time goes in v3:
time: 33.2 us; the launch traced here: 33.1 us
  Pallas kernels  31.8 us (96%)
  between operations  0.65 us (2%)
  other arithmetic  0.61 us (2%)
    pallas_call x1, Pallas kernels, body(): pl.pallas_call(functools.partial(density_kernel, n_blk, n_row), out_shape...  31.8 us

profile of v3, /device:TPU:0, one launch (start us, length us, event | category | flops | bytes accessed | tf_op | source)
XLA Modules:
  0.0 33.1 jit_solution(4865775127191890776)
XLA Ops:
  0.6 31.8 %shard_map.50 = (f32[1,1024]{1,0:T(1,128)S(1)}, f32[1,1024]{1,0:T(1,128)S(1)}, f32[1,1024]{1,0:T(1,128)S(1)}, f32[1,1024]{1,0:T(1,128)S(1)}) custom-call(bf16[1024,768]{1,0:T(8,128)(2,1)} %pool_hbm.1, bf16[64,768]{1,0:T(8,128)(2,1)} %target_hbm.1, bf16[64,768]{1,0:T(8,128)(2,1)} %ref_hbm.1), custom_call_target="tpu_custom_call" | custom-call | flops 1610612736 | bytes 1572864 | tf_op jit(solution)/shard_map/pallas_call | solution.py:408
  32.5 0.0 copy-start
  32.5 0.6 %subtract_divide_fusion = f32[1024]{0:T(1024)} fusion(f32[1024]{0:T(1024)S(1)} %bitcast.4, f32[1024]{0:T(1024)S(1)} %bitcast.5, f32[1024]{0:T(1024)S(1)} %bitcast.3), kind=kLoop, calls=%fused_computation | loop fusion | flops 2048 | bytes 16384 | tf_op jit(solution)/shard_map/div | solution.py:449
  33.1 0.0 copy-done
  (1 shorter events, 0.0 us)
Async XLA Ops:
  32.5 0.6 %copy-start = (f32[1,1024]{1,0:T(1,128)}, f32[1,1024]{1,0:T(1,128)S(1)}, u32[]{:S(2)}) copy-start(f32[1,1024]{1,0:T(1,128)S(1)} %sub.9) | copy-start | bytes 12292

commit v4 on v3

--- a/solution.py
+++ b/solution.py
@@ -170,9 +170,27 @@
     pool_load.wait()
     for load in own_loads:
         load.wait()
-    for k in range(2):
-        set_norms(place, k)
-    fold(place, 0)
+    def fold_early(which):
+        middle = (place > 0) & (place < length - 1)
+        first = jnp.minimum(place, 1)
+        if length <= 4:
+
+            @pl.when(middle)
+            def _():
+                fold(0, which, length)
+
+            @pl.when(jnp.logical_not(middle))
+            def _():
+                fold(first, which, length - 1)
+
+        else:
+
+            def early(origin, carry):
+                fold(origin, which)
+                return carry
+
+            stop = first + length - 1
+            lax.fori_loop(jnp.where(middle, 0, first), stop, early, 0)
 
     ones = jnp.ones((8, depth), jnp.bfloat16)
     tile = 256 if rows % 256 == 0 else rows
@@ -187,6 +205,7 @@
         pool_norms[:, pl.ds(at, tile)] = sums[0:1, :] * factor
         return carry
 
+    lax.fori_loop(0, rows // tile, norm_tile, 0)
     line_ticks = 2 * (length - 1)
     ticks = max(line_ticks, CHUNKS + 2)
 
@@ -227,28 +246,19 @@
                 row_relay(peer, i - 1, peer, x_send.at[peer, i - 1]).wait_recv()
                 core_copy(peer, i - 1).start()
 
-        @pl.when(i < rows // tile)
-        def _():
-            norm_tile(i, 0)
-
-        def norms_of(j, carry):
-            origin = place + (2 * j - 1) * step
-
-            @pl.when((i < line_ticks) & (origin >= 0) & (origin < length))
-            def _():
-                set_norms(origin, k)
-
-            return carry
-
-        lax.fori_loop(0, 2, norms_of, 0)
-
-        @pl.when((k == 1) & (place >= step) & (i < line_ticks - 1))
-        def _():
-            fold(place - step, 0)
-
-        @pl.when((k == 1) & (place + step < length) & (i < line_ticks - 1))
-        def _():
-            fold(place + step, 0)
+        @pl.when(i == ticks - 3)
+        def _():
+            def all_norms(j, carry):
+                origin = j // 2
+
+                @pl.when((origin - place < length - 1) & (place - origin < length - 1))
+                def _():
+                    set_norms(origin, lax.rem(j, 2))
+
+                return carry
+
+            lax.fori_loop(0, 2 * length, all_norms, 0)
+            fold_early(0)
 
         @pl.when(i == ticks - 2)
         def _():
@@ -261,25 +271,15 @@
 
                 lax.fori_loop(0, CHUNKS, arrived, 0)
 
-            first = jnp.minimum(place, 1)
-            if length <= 4:
-                fold(first, 1, length - 1)
-            else:
-
-                def early(origin, carry):
-                    fold(origin, 1)
-                    return carry
-
-                lax.fori_loop(first, first + length - 1, early, 0)
-
-            @pl.when((place > 0) & (place < length - 1))
-            def _():
-                fold(0, 1)
+            fold_early(1)
+
+        @pl.when((i >= line_ticks - 2) & (i < line_ticks) & ((place == 0) | (place == length - 1)))
+        def _():
+            set_norms(length - 1 - place, k)
 
         return carry
 
     lax.fori_loop(0, ticks, tick, 0)
-    lax.fori_loop(ticks, max(ticks, rows // tile), norm_tile, 0)
 
     @pl.when((place == 0) | (place == length - 1))
     def _():

time: 33.2 us -> 33 us (level)
  no operation moved by 1% of the time
where the time goes in v4:
time: 33 us; the launch traced here: 32.9 us
  Pallas kernels  31.6 us (96%)
  between operations  0.65 us (2%)
  other arithmetic  0.61 us (2%)
    pallas_call x1, Pallas kernels, body(): pl.pallas_call(functools.partial(density_kernel, n_blk, n_row), out_shape...  31.6 us

profile of v4, /device:TPU:0, one launch (start us, length us, event | category | flops | bytes accessed | tf_op | source)
XLA Modules:
  0.0 32.9 jit_solution(5670595049277501781)
XLA Ops:
  0.6 31.6 %shard_map.50 = (f32[1,1024]{1,0:T(1,128)S(1)}, f32[1,1024]{1,0:T(1,128)S(1)}, f32[1,1024]{1,0:T(1,128)S(1)}, f32[1,1024]{1,0:T(1,128)S(1)}) custom-call(bf16[1024,768]{1,0:T(8,128)(2,1)} %pool_hbm.1, bf16[64,768]{1,0:T(8,128)(2,1)} %target_hbm.1, bf16[64,768]{1,0:T(8,128)(2,1)} %ref_hbm.1), custom_call_target="tpu_custom_call" | custom-call | flops 1610612736 | bytes 1572864 | tf_op jit(solution)/shard_map/pallas_call | solution.py:408
  32.3 0.0 copy-start
  32.3 0.6 %subtract_divide_fusion = f32[1024]{0:T(1024)} fusion(f32[1024]{0:T(1024)S(1)} %bitcast.4, f32[1024]{0:T(1024)S(1)} %bitcast.5, f32[1024]{0:T(1024)S(1)} %bitcast.3), kind=kLoop, calls=%fused_computation | loop fusion | flops 2048 | bytes 16384 | tf_op jit(solution)/shard_map/div | solution.py:449
  32.9 0.0 copy-done
  (1 shorter events, 0.0 us)
Async XLA Ops:
  32.3 0.6 %copy-start = (f32[1,1024]{1,0:T(1,128)}, f32[1,1024]{1,0:T(1,128)S(1)}, u32[]{:S(2)}) copy-start(f32[1,1024]{1,0:T(1,128)S(1)} %sub.9) | copy-start | bytes 12292
